TPU v7x, 128 devices: a whole 4x4x4 slice. The times are simulated.
128 devices in a mesh: tensor: 4 (over x), dp: 16 (over z, y), outer: 2 (over core).
Axes of the slice: x: 4, y: 4, z: 4, core: 2. Of those that a mesh axis runs over, the one named last changes fastest.
Arguments:
- hidden_act: bfloat16 [8192, 14336], P(('dp', 'outer'), 'tensor'), may hold values from -6 to 6
- out_grad: bfloat16 [8192, 6144], P(('dp', 'outer')), may hold values from -6 to 6
- start_vectors: float32 [16, 6144], replicated, may hold values from -6 to 6
- kept_counts: int32 [4, 2, 16], P('tensor', 'outer', 'dp'), may hold values from 1 to 16, as said below
Outputs:
- synced_grad: bfloat16 [14336, 6144], P('tensor', 'outer')
Inputs may be any that keep to these rules, and one draw needn't show every extreme that they name: kept_counts[t, q, e] is how many atoms pod q keeps for piece (t, e); for some t and e every pod keeps 16, and some entry is 1.
All inputs are finite; a program needn't handle non-finite values.
Results may differ from a plain program's by a relative error of at most 0.039.
Values may be sent and summed in bfloat16 or wider, within the bound.
A program may use at most 256 MiB of HBM per device.

v0:
```python
import math

import jax
import jax.numpy as jnp
from jax import lax
from jax.sharding import PartitionSpec as P

TOK_DEV = 256
POWER = 2


PRECISE = lax.Precision.HIGHEST


def compress(owned_piece, start_vectors, kept_number):
    atom_count = start_vectors.shape[0]
    right_side = start_vectors
    left_side = None
    for repeat in range(POWER):
        left_side = lax.dot_general(
            right_side, owned_piece, (((1,), (1,)), ((), ())), precision=PRECISE
        )
        gram_matrix = jnp.dot(left_side, left_side.T, precision=PRECISE)
        ridge_term = 1e-05 * jnp.trace(gram_matrix) / atom_count
        factor = jnp.linalg.cholesky(
            gram_matrix + ridge_term * jnp.eye(atom_count, dtype=gram_matrix.dtype)
        )
        left_side = jax.scipy.linalg.solve_triangular(factor, left_side, lower=True)
        right_side = jnp.dot(left_side, owned_piece, precision=PRECISE)
    keep_mask = (jnp.arange(atom_count, dtype=jnp.int32) < kept_number)[:, None]
    left_atoms = jnp.where(keep_mask, left_side, 0.0).astype(jnp.bfloat16)
    right_atoms = jnp.where(keep_mask, right_side, 0.0).astype(jnp.bfloat16)
    return (left_atoms, right_atoms)


def shards(hidden_act, out_grad, start_vectors, kept_counts):
    feature_count = out_grad.shape[1]
    member_count = lax.axis_size("dp")
    pod_count = lax.axis_size("outer")
    pod_width = feature_count // pod_count
    grad_scale = 1.0 / math.sqrt(TOK_DEV * member_count)
    owned_piece = lax.psum_scatter(
        (
            lax.dot_general(
                hidden_act, out_grad, (((0,), (0,)), ((), ())), preferred_element_type=jnp.float32
            )
            * grad_scale
        ).astype(jnp.bfloat16),
        "dp",
        scatter_dimension=0,
        tiled=True,
    ).astype(jnp.float32)
    left_atoms, right_atoms = compress(owned_piece, start_vectors, kept_counts[0, 0, 0])
    pod_left, wide_right = (
        lax.all_gather(left_atoms, "outer", axis=0, tiled=True),
        lax.all_gather(right_atoms, "outer", axis=0, tiled=True),
    )
    pod_right = lax.dynamic_slice_in_dim(
        wide_right, lax.axis_index("outer") * pod_width, pod_width, 1
    )
    rebuilt = lax.dot_general(
        pod_left, pod_right, (((0,), (0,)), ((), ())), preferred_element_type=jnp.float32
    ).astype(jnp.bfloat16)
    return lax.all_gather(rebuilt, "dp", axis=0, tiled=True)


def solution(mesh):
    placed = (
        P(("dp", "outer"), "tensor"),
        P(("dp", "outer"), None),
        P(),
        P("tensor", "outer", "dp"),
    )
    return jax.shard_map(
        shards, mesh=mesh, in_specs=placed, out_specs=P("tensor", "outer"), check_vma=False
    )
```

profile of v0, /device:TPU:1, one launch (start us, length us, event | category | flops | bytes accessed | tf_op | source)
XLA Modules:
  0.0 469.0 jit_solution(2285681594774477591)
XLA Ops:
  6.5 1.9 copy-done
  8.4 19.3 %multiply_convert_fusion = bf16[3584,6144]{1,0:T(8,128)(2,1)} fusion(bf16[256,3584]{1,0:T(8,128)(2,1)} %param.7, bf16[256,6144]{1,0:T(8,128)(2,1)S(1)} %copy-done), kind=kOutput, calls=%fused_computation | convolution fusion | flops 11318329344 | bytes 49020928 | tf_op jit(solution)/shard_map/dot_general | solution.py:44
  27.8 0.0 reduce-scatter.2.cloned.1.call-update
  27.8 0.0 all-gather.2.cloned.1.call-start
  28.5 250.5 %reduce-scatter.2.cloned.1.call-done = bf16[224,6144]{1,0:T(8,128)(2,1)} async-done(((bf16[3584,6144]{1,0:T(8,128)(2,1)}), bf16[224,6144]{1,0:T(8,128)(2,1)}) %reduce-scatter.2.cloned.1.call-update) | async-done | bytes 2752528 | tf_op jit(solution)/shard_map/reduce_scatter | solution.py:42
  279.0 0.0 copy-done.3
  279.0 4.2 fusion.14
  283.2 0.8 select_reduce_fusion.2
  284.6 0.1 copy.7
  284.7 1.5 cholesky.44
  286.2 0.6 compare_reduce_fusion.1
  286.8 0.6 fusion.4
  287.5 1.2 custom-call.6
  288.7 0.2 fusion.2
  288.9 0.0 copy-done.2
  288.9 1.2 fusion.15
  290.1 2.2 fusion.16
  292.4 0.8 select_reduce_fusion.1
  293.8 0.1 copy.10
  293.9 1.5 cholesky.55
  295.4 0.6 compare_reduce_fusion
  296.0 0.6 fusion.5
  296.7 1.2 custom-call.7
  297.9 0.2 select_convert_fusion
  298.1 1.2 fusion
  299.3 2.3 all_gather.10
  301.6 1.8 all_gather.9
  303.5 1.6 convolution_convert_fusion
  305.1 0.0 all-gather.2.cloned.1.call-update
  305.1 137.7 %all-gather.2.cloned.1.call-done = bf16[3584,3072]{1,0:T(8,128)(2,1)} async-done(((bf16[224,3072]{1,0:T(8,128)(2,1)}), bf16[3584,3072]{1,0:T(8,128)(2,1)}) %all-gather.2.cloned.1.call-update) | async-done | bytes 22020112 | tf_op jit(solution)/shard_map/all_gather | solution.py:64
  442.8 19.3 %copy.15 = bf16[3584,3072]{1,0:T(8,128)(2,1)} copy(bf16[3584,3072]{1,0:T(8,128)(2,1)} %all-gather.2.cloned.1.call-done) | data formatting | bytes 44040192
  462.2 0.0 copy-done.1
  (12 shorter events, 0.1 us)
Async XLA Ops:
  6.5 1.9 copy-start
  6.5 272.5 %reduce-scatter.2.cloned.1.call-start = ((), (), s32[]{:S(2)}) async-start(), calls=%async_computation.1 | async-start | bytes 46792704 | tf_op jit(solution)/shard_map/reduce_scatter | solution.py:42
  27.8 251.3 %copy-start.3 = (f32[16,6144]{1,0:T(8,128)S(1)}, f32[16,6144]{1,0:T(8,128)}, u32[]{:S(2)}) copy-start(f32[16,6144]{1,0:T(8,128)} %param.9) | copy-start | bytes 1179652
  27.8 415.0 %all-gather.2.cloned.1.call-start = ((), (), s32[]{:S(2)}) async-start(), calls=%async_computation.2 | async-start | bytes 23396352 | tf_op jit(solution)/shard_map/all_gather | solution.py:64
  279.0 9.9 %copy-start.2 = (bf16[224,6144]{1,0:T(8,128)(2,1)S(1)}, bf16[224,6144]{1,0:T(8,128)(2,1)}, u32[]{:S(2)}) copy-start(bf16[224,6144]{1,0:T(8,128)(2,1)} %reduce-scatter.2.cloned.1.call-done) | copy-start | bytes 8257540
  442.8 19.4 %copy-start.1 = (bf16[256,6144]{1,0:T(8,128)(2,1)S(1)}, bf16[256,6144]{1,0:T(8,128)(2,1)}, u32[]{:S(2)}) copy-start(bf16[256,6144]{1,0:T(8,128)(2,1)} %param.8) | copy-start | bytes 9437188
Sparse Core Ops, SparseCore 0:
  27.9 251.0 reduce-scatter.1
  305.2 137.5 all-gather.1
where the time goes:
time: 469 us
  waiting for transfers between devices  388 us (83%)
  matrix products  31.7 us (7%)
  local copies, waits for them, and re-layouts  21.4 us (5%)
  between operations  15.5 us (3%)
  other arithmetic  8.05 us (2%)
    reduce_scatter x1, waiting for transfers between devices, shards(): lax.psum_scatter((lax.dot_general(hidden_act, out_grad, (((0,), (0,)), ((...  250 us
    all_gather x1, waiting for transfers between devices, shards(): return lax.all_gather(rebuilt, 'dp', axis=0, tiled=True)  138 us
    unnamed x9, local copies, waits for them, and re-layouts  21.3 us
    dot_general x1, matrix products, shards(): lax.dot_general(hidden_act, out_grad, (((0,), (0,)), ((), ())), preferred...  19.3 us
  transfers between devices with their start and end apart: 2, of which 2 were waited for; matrix products, arithmetic and copies ran while one was open for 0% of the time, Pallas kernels for 0%

commit v1 on v0

v1 whole, which is shorter than its diff:
```python
import math

import jax
import jax.numpy as jnp
from jax import lax
from jax.sharding import PartitionSpec as P

TOK_DEV = 256
POWER = 2


PRECISE = lax.Precision.HIGHEST


def orthonormal(left_side):
    atom_count = left_side.shape[0]
    gram_matrix = jnp.dot(left_side, left_side.T, precision=PRECISE)
    ridge_term = 1e-05 * jnp.trace(gram_matrix) / atom_count
    factor = jnp.linalg.cholesky(
        gram_matrix + ridge_term * jnp.eye(atom_count, dtype=gram_matrix.dtype)
    )
    return jax.scipy.linalg.solve_triangular(factor, left_side, lower=True)


def shards(hidden_act, out_grad, start_vectors, kept_counts):
    token_count, feature_count = out_grad.shape
    atom_count = start_vectors.shape[0]
    member_count = lax.axis_size("dp")
    pod_count = lax.axis_size("outer")
    pod_width = feature_count // pod_count
    own_rows = hidden_act.shape[1] // member_count
    grad_scale = 1.0 / math.sqrt(TOK_DEV * member_count)
    hidden = hidden_act.reshape(token_count, member_count, own_rows)
    hidden_wide = hidden.astype(jnp.float32)
    grad_wide = out_grad.astype(jnp.float32)

    token_side = lax.dot_general(
        start_vectors, grad_wide, (((1,), (1,)), ((), ())), precision=PRECISE
    )
    left_side = jnp.einsum("at,ter->ear", token_side, hidden_wide, precision=PRECISE)
    for repeat in range(POWER):
        left_side = lax.psum_scatter(left_side, "dp", scatter_dimension=0, tiled=True)[0] * grad_scale
        left_side = orthonormal(left_side)
        if repeat == POWER - 1:
            keep_mask = jnp.arange(atom_count, dtype=jnp.int32) < kept_counts[0, 0, 0]
            left_side = jnp.where(keep_mask[:, None], left_side, 0.0)
        all_left = lax.all_gather(left_side, "dp", axis=0)
        token_side = jnp.einsum("ear,ter->eat", all_left, hidden_wide, precision=PRECISE) * grad_scale
        token_side = token_side.reshape(member_count * atom_count, token_count)
        right_part = jnp.dot(
            token_side.astype(jnp.bfloat16), out_grad, preferred_element_type=jnp.float32
        ).astype(jnp.bfloat16)
        if repeat < POWER - 1:
            right_side = lax.psum(right_part, "dp")
            token_side = lax.dot_general(
                right_side, out_grad, (((1,), (1,)), ((), ())), preferred_element_type=jnp.float32
            ).reshape(member_count, atom_count, token_count)
            left_side = jnp.einsum("eat,ter->ear", token_side, hidden_wide, precision=PRECISE)
        else:
            right_side = lax.psum_scatter(right_part, "dp", scatter_dimension=0, tiled=True)
    all_left = lax.all_gather(all_left.astype(jnp.bfloat16), "outer", axis=1)
    both_right = lax.all_to_all(right_side, "outer", split_axis=1, concat_axis=0, tiled=True)
    all_right = lax.all_gather(both_right, "dp", axis=0)
    rebuilt = jnp.einsum(
        "ekr,ekc->erc",
        all_left.reshape(member_count, pod_count * atom_count, own_rows),
        all_right.reshape(member_count, pod_count * atom_count, pod_width),
        preferred_element_type=jnp.float32,
    )
    return rebuilt.reshape(member_count * own_rows, pod_width).astype(jnp.bfloat16)


def solution(mesh):
    placed = (
        P(("dp", "outer"), "tensor"),
        P(("dp", "outer"), None),
        P(),
        P("tensor", "outer", "dp"),
    )
    return jax.shard_map(
        shards, mesh=mesh, in_specs=placed, out_specs=P("tensor", "outer"), check_vma=False
    )
```

time: 469 us -> 480 us (1.023)
  blocking collectives: 4.19 us -> 42.8 us
  waiting for transfers between devices: 388 us -> 370 us
  local copies, waits for them, and re-layouts: 21.4 us -> 5.06 us
  matrix products: 31.7 us -> 37.3 us
    reduce_scatter x1, waiting for transfers between devices: 250 us -> 80.7 us  [shards(): lax.psum_scatter(right_part, 'dp', scatter_dimension=0, tiled=True)]
    unnamed x2 -> x7, waiting for transfers between devices: 0.03 us -> 143 us
    psum x0 -> x1, waiting for transfers between devices: none -> 102 us  [shards(): right_side = lax.psum(right_part, 'dp')]
    all_gather x1, waiting for transfers between devices: 138 us -> 44.6 us  [shards(): all_right = lax.all_gather(both_right, 'dp', axis=0)]
    all_gather x2 -> x3, blocking collectives: 4.19 us -> 36.3 us  [the longest x2 34.1 us: shards(): all_left = lax.all_gather(left_side, 'dp', axis=0)]
    unnamed x9, local copies, waits for them, and re-layouts: 21.3 us -> 3.98 us
    all_to_all x0 -> x1, blocking collectives: none -> 6.55 us  [shards(): lax.all_to_all(right_side, 'outer', split_axis=1, concat_axis=0, tiled=True)]
    dot_general x8 -> x11, matrix products: 31.3 us -> 35.5 us  [the longest x1 12.3 us: shards(): jnp.einsum('ekr,ekc->erc', all_left.reshape(member_count, pod_count * ato...]
  transfers between devices with their start and end apart: 2 -> 5, of which waited for: 2 -> 5; matrix products, arithmetic and copies ran while one was open for 0% -> 0% of each run, Pallas kernels for 0% -> 0%
where the time goes in v1:
time: 480 us; the launch traced here: 479 us
  waiting for transfers between devices  370 us (77%)
  blocking collectives  42.8 us (9%)
  matrix products  37.3 us (8%)
  between operations  15.2 us (3%)
  other arithmetic  8.07 us (2%)
  local copies, waits for them, and re-layouts  5.06 us (1%)
    unnamed x7, waiting for transfers between devices  143 us
    psum x1, waiting for transfers between devices, shards(): right_side = lax.psum(right_part, 'dp')  102 us
    reduce_scatter x1, waiting for transfers between devices, shards(): lax.psum_scatter(right_part, 'dp', scatter_dimension=0, tiled=True)  80.7 us
    all_gather x1, waiting for transfers between devices, shards(): all_right = lax.all_gather(both_right, 'dp', axis=0)  44.6 us
    all_gather x2, blocking collectives, shards(): all_left = lax.all_gather(left_side, 'dp', axis=0)  34.1 us
    dot_general x1, matrix products, shards(): jnp.einsum('ekr,ekc->erc', all_left.reshape(member_count, pod_count * ato...  12.3 us
  transfers between devices with their start and end apart: 5, of which 5 were waited for; matrix products, arithmetic and copies ran while one was open for 0% of the time, Pallas kernels for 0%

profile of v1, /device:TPU:1, one launch (start us, length us, event | category | flops | bytes accessed | tf_op | source)
XLA Modules:
  0.0 478.9 jit_solution(2624609807157937716)
XLA Ops:
  6.5 3.9 copy.24
  10.5 2.5 convolution_bitcast_fusion.1
  13.1 2.3 convolution_bitcast_fusion
  15.4 73.8 %reduce-scatter.10.cloned.1.call-done = f32[1,16,224]{2,1,0:T(8,128)} async-done(((f32[16,16,224]{2,1,0:T(8,128)}), f32[1,16,224]{2,1,0:T(8,128)}) %reduce-scatter.10.cloned.1.call-update) | async-done | bytes 14352
  89.2 1.5 select_reduce_fusion.2
  91.5 1.5 cholesky.44
  92.9 0.6 compare_reduce_fusion.1
  93.6 0.6 fusion.13
  94.2 1.2 custom-call.6
  95.5 0.9 fusion.5
  96.4 17.0 %all-gather = f32[256,224]{1,0:T(8,128)S(1)} all-gather(f32[16,224]{1,0:T(8,128)S(1)} %fusion.5), channel_id=2, replica_groups=mesh['tensor'=4,'dp'=16,'outer'=2] {'dp'}, dimensions={0}, use_global_device_ids=true | all-gather | bytes 243712 | tf_op jit(solution)/shard_map/all_gather | solution.py:47
  113.4 2.3 fusion
  115.8 2.7 convolution_convert_fusion.2
  118.5 101.8 %all-reduce.4.cloned.1.call-done = bf16[256,6144]{1,0:T(8,128)(2,1)} async-done(((bf16[256,6144]{1,0:T(8,128)(2,1)}), bf16[256,6144]{1,0:T(8,128)(2,1)}) %all-reduce.4.cloned.1.call-update) | async-done | bytes 3145744 | tf_op jit(solution)/shard_map/psum | solution.py:54
  220.3 3.0 fusion.29
  223.4 2.2 fusion.30
  226.3 69.3 %reduce-scatter.12.cloned.1.call-done = f32[1,16,224]{2,1,0:T(8,128)} async-done(((f32[16,16,224]{2,1,0:T(8,128)}), f32[1,16,224]{2,1,0:T(8,128)}) %reduce-scatter.12.cloned.1.call-update) | async-done | bytes 14352
  295.7 1.5 select_reduce_fusion.1
  298.0 1.5 cholesky.55
  299.5 0.6 compare_reduce_fusion
  300.1 0.6 fusion.14
  300.8 1.2 custom-call.7
  302.0 0.9 convolution_select_fusion
  302.9 17.1 %all-gather.1 = f32[256,224]{1,0:T(8,128)S(1)} all-gather(f32[16,224]{1,0:T(8,128)S(1)} %convolution_select_fusion), channel_id=3, replica_groups=mesh['tensor'=4,'dp'=16,'outer'=2] {'dp'}, dimensions={0}, use_global_device_ids=true | all-gather | bytes 243712 | tf_op jit(solution)/shard_map/all_gather | solution.py:47
  320.0 2.3 fusion.1
  322.3 2.7 convolution_convert_fusion.1
  325.1 80.7 %reduce-scatter.8.cloned.1.call-done = bf16[16,6144]{1,0:T(8,128)(2,1)} async-done(((bf16[256,6144]{1,0:T(8,128)(2,1)}), bf16[16,6144]{1,0:T(8,128)(2,1)}) %reduce-scatter.8.cloned.1.call-update) | async-done | bytes 196624 | tf_op jit(solution)/shard_map/reduce_scatter | solution.py:60
  405.7 0.9 copy.36
  406.7 6.5 %all_to_all.16 = bf16[16,2,3072]{2,0,1:T(8,128)(2,1)} all-to-all(bf16[16,2,3072]{2,0,1:T(8,128)(2,1)S(1)} %bitcast.79), channel_id=1, replica_groups=mesh['tensor'=4,'dp'=16,'outer'=2] {'outer'}, dimensions={1} | all-to-all | bytes 393216 | tf_op jit(solution)/shard_map/all_to_all | solution.py:62
  413.3 2.2 all-gather.2
  415.5 44.6 %all-gather.5.cloned.1.call-done = bf16[16,32,3072]{2,1,0:T(8,128)(2,1)} async-done(((bf16[1,32,3072]{2,1,0:T(8,128)(2,1)}), bf16[16,32,3072]{2,1,0:T(8,128)(2,1)}) %all-gather.5.cloned.1.call-update) | async-done | bytes 3145744 | tf_op jit(solution)/shard_map/all_gather | solution.py:63
  460.0 12.3 %convolution_convert_fusion = bf16[16,224,3072]{2,1,0:T(8,128)(2,1)} fusion(bf16[16,32,224]{2,1,0:T(8,128)(2,1)S(1)} %all-gather.2, bf16[16,32,3072]{2,1,0:T(8,128)(2,1)} %all-gather.5.cloned.1.call-done), kind=kOutput, calls=%fused_computation | convolution fusion | flops 715653120 | bytes 25395200 | tf_op jit(solution)/shard_map/ekr,ekc->erc/dot_general | solution.py:64
  (28 shorter events, 0.5 us)
Async XLA Ops:
  6.5 4.0 copy-start
  6.5 4.0 copy-start.3
  6.5 82.6 %reduce-scatter.10.cloned.1.call-start = ((), (), s32[]{:S(2)}) async-start(), calls=%async_computation.7 | async-start | bytes 278528
  10.5 2.6 copy-start.1
  15.3 205.0 %all-reduce.4.cloned.1.call-start = ((), (), s32[]{:S(2)}) async-start(), calls=%async_computation.4 | async-start | bytes 6291456 | tf_op jit(solution)/shard_map/psum | solution.py:54
  118.5 177.2 %reduce-scatter.12.cloned.1.call-start = ((), (), s32[]{:S(2)}) async-start(), calls=%async_computation.8 | async-start | bytes 278528
  220.3 3.0 copy-start.2
  225.6 180.1 %reduce-scatter.8.cloned.1.call-start = ((), (), s32[]{:S(2)}) async-start(), calls=%async_computation.5 | async-start | bytes 3342336 | tf_op jit(solution)/shard_map/reduce_scatter | solution.py:60
  325.0 135.0 %all-gather.5.cloned.1.call-start = ((), (), s32[]{:S(2)}) async-start(), calls=%async_computation.6 | async-start | bytes 3342336 | tf_op jit(solution)/shard_map/all_gather | solution.py:63
Sparse Core Ops, SparseCore 0:
  15.5 73.6 reduce-scatter.9
  118.6 101.6 all-reduce.3
  225.8 69.8 reduce-scatter.11
  325.1 80.5 reduce-scatter.7
  413.4 46.5 all-gather.4

commit v2 on v0

v2 whole, which is shorter than its diff:
```python
import functools
import math

import jax
import jax.numpy as jnp
from jax import lax
from jax.experimental import pallas as pl
from jax.experimental.pallas import tpu as pltpu
from jax.sharding import PartitionSpec as P

POWER = 2
SIDE = 4
LANES = 128
VMEM_BYTES = 48 * 1024 * 1024

F32 = jnp.float32
BF16 = jnp.bfloat16
NT = (((1,), (1,)), ((), ()))
TN = (((0,), (0,)), ((), ()))


def dot_nt(a, b):
    return lax.dot_general(a, b, NT, preferred_element_type=F32)


def dot_nn(a, b):
    return jnp.dot(a, b, preferred_element_type=F32)


def split2(x):
    high = x.astype(BF16)
    return jnp.concatenate([high, (x - high.astype(F32)).astype(BF16)], axis=0)


def split3(x):
    high = x.astype(BF16)
    rest = x - high.astype(F32)
    middle = rest.astype(BF16)
    low = (rest - middle.astype(F32)).astype(BF16)
    return jnp.concatenate([high, middle, low], axis=0)


def fold(x, times):
    rows = x.shape[0] // times
    total = x[:rows]
    for i in range(1, times):
        total = total + x[i * rows : (i + 1) * rows]
    return total


def orthonormal(left):
    atoms = left.shape[0]
    gram = lax.dot_general(left, left, NT, precision=lax.Precision.HIGHEST, preferred_element_type=F32)
    row = lax.broadcasted_iota(jnp.int32, (atoms, atoms), 0)
    col = lax.broadcasted_iota(jnp.int32, (atoms, atoms), 1)
    diagonal = row == col
    ridge = 1e-05 * jnp.sum(jnp.where(diagonal, gram, 0.0)) / atoms
    gram = gram + jnp.where(diagonal, ridge, 0.0)
    below = lax.broadcasted_iota(jnp.int32, (atoms, 1), 0)
    for j in range(atoms - 1):
        factor = jnp.where(below > j, gram[:, j : j + 1] / gram[j : j + 1, j : j + 1], 0.0)
        left = left - factor * left[j : j + 1]
        gram = gram - factor * gram[j : j + 1]
    pivots = jnp.sum(jnp.where(diagonal, gram, 0.0), axis=1, keepdims=True)
    return left / jnp.sqrt(pivots)


class Ring:
    def __init__(self, place, right, left):
        self.place, self.right, self.left = place, right, left

    def at(self, shift):
        return lax.rem(self.place + shift + SIDE, SIDE)


class Sems:
    def __init__(self, send, recv):
        self.send, self.recv, self.used = send, recv, 0

    def take(self, count):
        first = self.used
        self.used += count
        return first


def chain(
    members,
    atoms,
    own_rows,
    scale,
    h_hbm,
    o_hbm,
    s_hbm,
    kept_ref,
    f2,
    left_out,
    h_v,
    o_v,
    s_v,
    hp,
    o_a,
    o_b,
    zs,
    zr,
    ls,
    lr,
    u_y,
    u_z,
    v_a,
    v_b,
    va_full,
    vb_full,
    w_a,
    w_b,
    rs_v,
    rs_w,
    x_send,
    f1,
    send_sems,
    recv_sems,
    local_sems,
):
    me = lax.axis_index("dp")
    pod = lax.axis_index("outer")
    y, z = lax.rem(me, SIDE), me // SIDE
    ring_y = Ring(y, z * SIDE + lax.rem(y + 1, SIDE), z * SIDE + lax.rem(y + 3, SIDE))
    ring_z = Ring(z, lax.rem(z + 1, SIDE) * SIDE + y, lax.rem(z + 3, SIDE) * SIDE + y)
    tokens, features = o_v.shape
    half = features // 2
    quarter = half // SIDE
    padded = hp.shape[2]
    sems = Sems(send_sems, recv_sems)
    sent = []

    def remote(src, dst, k, dp=None, outer=None):
        device = {"dp": dp} if outer is None else {"outer": outer}
        return pltpu.make_async_remote_copy(
            src_ref=src,
            dst_ref=dst,
            send_sem=sems.send.at[k],
            recv_sem=sems.recv.at[k],
            device_id=device,
            device_id_type=pl.DeviceIdType.MESH,
        )

    def member(shift):
        return lax.rem(me + shift + members, members)

    load_o = pltpu.make_async_copy(o_hbm, o_v, local_sems.at[0])
    load_h = pltpu.make_async_copy(h_hbm, h_v, local_sems.at[1])
    load_s = pltpu.make_async_copy(s_hbm, s_v, local_sems.at[2])
    load_s.start()
    load_o.start()
    load_h.start()
    own_a = pltpu.make_async_copy(
        o_hbm.at[:, pl.ds(pl.multiple_of(y * quarter, quarter), quarter)], o_a.at[y], local_sems.at[3]
    )
    own_b = pltpu.make_async_copy(
        o_hbm.at[:, pl.ds(pl.multiple_of(half + z * quarter, quarter), quarter)], o_b.at[z], local_sems.at[4]
    )
    own_a.start()
    own_b.start()

    barrier = pltpu.get_barrier_semaphore()

    def greet(k, carry):
        pl.semaphore_signal(
            barrier, inc=1, device_id={"dp": member(k)}, device_id_type=pl.DeviceIdType.MESH
        )
        return carry

    lax.fori_loop(1, members, greet, 0)
    pl.semaphore_signal(barrier, inc=1, device_id={"outer": 1 - pod}, device_id_type=pl.DeviceIdType.MESH)
    pl.semaphore_wait(barrier, members)

    regroup = []
    for shift in (1, 3, 2):
        for ring, first, buf, dest in (
            (ring_y, 0, o_a, z * SIDE + ring_y.at(shift)),
            (ring_z, half, o_b, ring_z.at(shift) * SIDE + y),
        ):
            k = sems.take(1)
            begin = pl.multiple_of(first + ring.at(shift) * quarter, quarter)
            copy = remote(o_hbm.at[:, pl.ds(begin, quarter)], buf.at[ring.place], k, dp=dest)
            copy.start()
            sent.append(copy)
            regroup.append(remote(buf.at[ring.at(-shift)], buf.at[ring.at(-shift)], k, dp=dest))

    load_s.wait()
    start3 = split3(s_v[...])
    load_o.wait()
    token_side = dot_nt(start3, o_v[...])
    load_h.wait()
    for e in range(members):
        block = h_v[:, e * own_rows : (e + 1) * own_rows]
        hp[e] = jnp.concatenate([block, jnp.zeros((tokens, padded - own_rows), BF16)], axis=1)
    first3 = split3(fold(token_side, 3))
    for e in range(members):
        zs[0, e] = fold(dot_nn(first3, hp[e]), 3) * scale

    def exchange(src_of, dst, base):
        def go(k, carry):
            to = member(k)
            remote(src_of(to), dst.at[me], base + k, dp=to).start()
            return carry

        def arrive(k, carry):
            came = member(-k)
            remote(dst.at[came], dst.at[came], base + k, dp=came).wait_recv()
            return carry

        lax.fori_loop(1, members, go, 0)
        return lambda: lax.fori_loop(1, members, arrive, 0)

    def sent_exchange(src, base):
        def done(k, carry):
            remote(src, src, base + k, dp=member(k)).wait_send()
            return carry

        lax.fori_loop(1, members, done, 0)

    def gather_start(buf, ring):
        base = sems.take(6)
        rows = buf.shape[1] // 2

        def part(slot, which):
            return buf.at[slot, pl.ds(which * rows, rows)]

        def copy(slot, which, to, k):
            c = remote(part(slot, which), part(slot, which), base + k, dp=to)
            c.start()
            sent.append(c)

        copy(ring.place, 0, ring.right, 0)
        copy(ring.place, 1, ring.left, 2)
        copy(ring.place, 1, ring.right, 1)
        copy(ring.place, 0, ring.left, 3)

        def arrived(slot, which, k):
            remote(part(slot, which), part(slot, which), base + k, dp=ring.right).wait_recv()

        def forward():
            arrived(ring.at(-1), 0, 0)
            copy(ring.at(-1), 0, ring.right, 4)
            arrived(ring.at(1), 1, 2)
            copy(ring.at(1), 1, ring.left, 5)

        def finish():
            arrived(ring.at(-1), 1, 1)
            arrived(ring.at(1), 0, 3)
            arrived(ring.at(2), 0, 4)
            arrived(ring.at(2), 1, 5)

        return forward, finish

    def gather(pairs):
        steps = [gather_start(buf, ring) for buf, ring in pairs]
        for forward, _ in steps:
            forward()
        for _, finish in steps:
            finish()

    def sum_start(parts, land, ring):
        base = sems.take(6)
        rows = parts.shape[1] // 2

        def part(slot, which):
            return parts.at[slot, pl.ds(which * rows, rows)]

        def copy(src, place, to, k):
            c = remote(src, land.at[place], base + k, dp=to)
            c.start()
            sent.append(c)

        copy(part(ring.at(2), 0), 0, ring.right, 0)
        copy(part(ring.at(2), 1), 2, ring.left, 1)
        copy(part(ring.at(1), 1), 1, ring.right, 2)
        copy(part(ring.at(-1), 0), 3, ring.left, 3)

        def arrived(place, k):
            remote(land.at[place], land.at[place], base + k, dp=ring.right).wait_recv()

        def value(slot, which):
            return parts[slot, pl.ds(which * rows, rows)].astype(F32)

        def forward():
            arrived(0, 0)
            land[6] = (land[0].astype(F32) + value(ring.at(1), 0)).astype(BF16)
            copy(land.at[6], 4, ring.right, 4)
            arrived(2, 1)
            land[7] = (land[2].astype(F32) + value(ring.at(-1), 1)).astype(BF16)
            copy(land.at[7], 5, ring.left, 5)

        def finish():
            arrived(1, 2)
            arrived(3, 3)
            arrived(4, 4)
            arrived(5, 5)
            top = value(ring.place, 0) + land[4].astype(F32) + land[3].astype(F32)
            low = value(ring.place, 1) + land[1].astype(F32) + land[5].astype(F32)
            return jnp.concatenate([top, low], axis=0)

        return forward, finish

    def ring_sums(triples):
        steps = [sum_start(*triple) for triple in triples]
        for forward, _ in steps:
            forward()
        return [finish() for _, finish in steps]

    group = members * atoms // SIDE
    for step in range(POWER):
        last = step == POWER - 1
        base = sems.take(members)
        arrive = exchange(lambda i: zs.at[step, i], zr.at[step], base)
        sent_z = base
        zr[step, me] = zs[step, me]
        arrive()
        left = orthonormal(jnp.sum(zr[step], axis=0))
        if last:
            atom = lax.broadcasted_iota(jnp.int32, (atoms, 1), 0)
            left = jnp.where(atom < kept_ref[0, 0], left, 0.0)
        pair = split2(left)
        ls[step] = pair
        lr[step, me] = pair
        base = sems.take(members)
        arrive = exchange(lambda i: ls.at[step], lr.at[step], base)
        arrive()
        sent_exchange(zs.at[step, 0], sent_z)
        sent_exchange(ls.at[step], base)
        if last:
            own_left = pltpu.make_async_copy(
                lr.at[step, :, pl.ds(0, atoms)], left_out.at[:, pod], local_sems.at[5]
            )
            own_left.start()
            left_k = sems.take(1)
            other_left = remote(
                lr.at[step, :, pl.ds(0, atoms)], left_out.at[:, pod], left_k, outer=1 - pod
            )
            other_left.start()
            sent.append(other_left)

        for e in range(members):
            block = (fold(dot_nt(lr[step, e], hp[e]), 2) * scale).astype(BF16)
            u_y[step, y, e * atoms : (e + 1) * atoms] = block
            u_z[step, z, e * atoms : (e + 1) * atoms] = block
        gather([(u_y.at[step], ring_y), (u_z.at[step], ring_z)])

        if step == 0:
            own_a.wait()
            own_b.wait()
            for copy in regroup:
                copy.wait_recv()

        for u, o, v in ((u_y, o_a, v_a), (u_z, o_b, v_b)):
            total = dot_nn(u[step, 0], o[0])
            for c in range(1, SIDE):
                total = total + dot_nn(u[step, c], o[c])
            total = total.astype(BF16)
            for c in range(SIDE):
                v[step, c] = total[c * group : (c + 1) * group]
        sum_a, sum_b = ring_sums(
            [(v_a.at[step], rs_v.at[step, 0], ring_z), (v_b.at[step], rs_v.at[step, 1], ring_y)]
        )
        if last:
            break
        va_full[z] = sum_a.astype(BF16)
        vb_full[y] = sum_b.astype(BF16)
        gather([(va_full, ring_z), (vb_full, ring_y)])
        for v, o, w in ((va_full, o_a, w_a), (vb_full, o_b, w_b)):
            whole = v[...].reshape(members * atoms, quarter)
            for c in range(SIDE):
                w[c] = dot_nt(whole, o[c]).astype(BF16)
        sum_a, sum_b = ring_sums([(w_a, rs_w.at[0], ring_y), (w_b, rs_w.at[1], ring_z)])
        token_side = sum_a + sum_b
        for e in range(members):
            pair = split2(token_side[e * atoms : (e + 1) * atoms])
            zs[step + 1, e] = fold(dot_nn(pair, hp[e]), 2) * scale

    per_row = group // atoms
    mine = jnp.where(pod == 0, sum_a, sum_b).astype(BF16).reshape(per_row, atoms, quarter)
    other = jnp.where(pod == 0, sum_b, sum_a).astype(BF16).reshape(per_row, atoms, quarter)
    row_place = z + pod * (y - z)
    col_place = y + pod * (z - y)
    rows_ring = Ring(
        row_place,
        ring_z.right + pod * (ring_y.right - ring_z.right),
        ring_z.left + pod * (ring_y.left - ring_z.left),
    )
    cols_ring = Ring(
        col_place,
        ring_y.right + pod * (ring_z.right - ring_y.right),
        ring_y.left + pod * (ring_z.left - ring_y.left),
    )
    x_send[...] = other
    k = sems.take(1)
    cross = remote(x_send, f1.at[col_place, :, pod], k, outer=1 - pod)
    cross.start()
    sent.append(cross)
    f1[row_place, :, pod] = mine
    remote(f1.at[row_place, :, 1 - pod], f1.at[row_place, :, 1 - pod], k, outer=1 - pod).wait_recv()
    gather([(f1, rows_ring)])
    own_cols = pltpu.make_async_copy(f1, f2.at[col_place], local_sems.at[6])
    own_cols.start()
    own_cols.wait()
    gather([(f2, cols_ring)])
    own_left.wait()
    other_left.wait_recv()
    for copy in sent:
        copy.wait_send()


def rebuild_kernel(left_ref, right_ref, out_ref):
    own_rows = out_ref.shape[0]
    left = left_ref[0].reshape(-1, left_ref.shape[-1])[:, :own_rows]
    width = right_ref.shape[-1]
    for c in range(right_ref.shape[0]):
        right = right_ref[c, 0].reshape(left.shape[0], width)
        out_ref[:, c * width : (c + 1) * width] = lax.dot_general(
            left, right, TN, preferred_element_type=F32
        ).astype(BF16)


def shards(hidden_act, out_grad, start_vectors, kept_counts):
    tokens, features = out_grad.shape
    atoms = start_vectors.shape[0]
    members = lax.axis_size("dp")
    pods = lax.axis_size("outer")
    hidden_rows = hidden_act.shape[1]
    own_rows = hidden_rows // members
    padded = -(-own_rows // LANES) * LANES
    quarter = features // 2 // SIDE
    group = members * atoms // SIDE
    per_row = group // atoms
    scale = 1.0 / math.sqrt(tokens * members)
    any_space = pl.BlockSpec(memory_space=pl.ANY)
    sem_count = 6 + 4 * members + 2 + 6 * 14
    right_atoms, left_atoms = pl.pallas_call(
        functools.partial(chain, members, atoms, own_rows, scale),
        out_shape=(
            jax.ShapeDtypeStruct((SIDE, SIDE, per_row, pods, atoms, quarter), BF16),
            jax.ShapeDtypeStruct((members, pods, atoms, padded), BF16),
        ),
        in_specs=[any_space, any_space, any_space, pl.BlockSpec(memory_space=pltpu.SMEM)],
        out_specs=(any_space, any_space),
        scratch_shapes=[
            pltpu.VMEM((tokens, hidden_rows), BF16),
            pltpu.VMEM((tokens, features), BF16),
            pltpu.VMEM((atoms, features), F32),
            pltpu.VMEM((members, tokens, padded), BF16),
            pltpu.VMEM((SIDE, tokens, quarter), BF16),
            pltpu.VMEM((SIDE, tokens, quarter), BF16),
            pltpu.VMEM((POWER, members, atoms, padded), F32),
            pltpu.VMEM((POWER, members, atoms, padded), F32),
            pltpu.VMEM((POWER, 2 * atoms, padded), BF16),
            pltpu.VMEM((POWER, members, 2 * atoms, padded), BF16),
            pltpu.VMEM((POWER, SIDE, members * atoms, tokens), BF16),
            pltpu.VMEM((POWER, SIDE, members * atoms, tokens), BF16),
            pltpu.VMEM((POWER, SIDE, group, quarter), BF16),
            pltpu.VMEM((POWER, SIDE, group, quarter), BF16),
            pltpu.VMEM((SIDE, group, quarter), BF16),
            pltpu.VMEM((SIDE, group, quarter), BF16),
            pltpu.VMEM((SIDE, members * atoms, tokens), BF16),
            pltpu.VMEM((SIDE, members * atoms, tokens), BF16),
            pltpu.VMEM((POWER, 2, 8, group // 2, quarter), BF16),
            pltpu.VMEM((2, 8, members * atoms // 2, tokens), BF16),
            pltpu.VMEM((per_row, atoms, quarter), BF16),
            pltpu.VMEM((SIDE, per_row, pods, atoms, quarter), BF16),
            pltpu.SemaphoreType.DMA((sem_count,)),
            pltpu.SemaphoreType.DMA((sem_count,)),
            pltpu.SemaphoreType.DMA((7,)),
        ],
        compiler_params=pltpu.CompilerParams(
            collective_id=0, has_side_effects=True, vmem_limit_bytes=VMEM_BYTES
        ),
        name="power_chain",
    )(hidden_act, out_grad, start_vectors, kept_counts.reshape(1, 1))
    return pl.pallas_call(
        rebuild_kernel,
        out_shape=jax.ShapeDtypeStruct((hidden_rows, features // pods), BF16),
        grid=(members,),
        in_specs=[
            pl.BlockSpec((1, pods, atoms, padded), lambda e: (e, 0, 0, 0)),
            pl.BlockSpec((SIDE, 1, pods, atoms, quarter), lambda e: (0, e, 0, 0, 0)),
        ],
        out_specs=pl.BlockSpec((own_rows, features // pods), lambda e: (e, 0)),
        compiler_params=pltpu.CompilerParams(vmem_limit_bytes=VMEM_BYTES),
        name="rebuild",
    )(left_atoms, right_atoms.reshape(SIDE, members, pods, atoms, quarter))


def solution(mesh):
    placed = (
        P(("dp", "outer"), "tensor"),
        P(("dp", "outer"), None),
        P(),
        P("tensor", "outer", "dp"),
    )
    return jax.shard_map(
        shards, mesh=mesh, in_specs=placed, out_specs=P("tensor", "outer"), check_vma=False
    )
```

time: 469 us -> 146 us (0.31)
  waiting for transfers between devices: 388 us -> 0 us
  Pallas kernels: 0 us -> 143 us
  matrix products: 31.7 us -> 0 us
  local copies, waits for them, and re-layouts: 21.4 us -> 2.49 us
  between operations: 15.5 us -> 0.67 us
  other arithmetic: 8.05 us -> 0 us
    reduce_scatter x1 -> x0, waiting for transfers between devices: 250 us -> none  [shards(): lax.psum_scatter((lax.dot_general(hidden_act, out_grad, (((0,), (0,)), ((...]
    pallas_call x0 -> x2, Pallas kernels: none -> 143 us  [the longest x1 129 us: shards(): pl.pallas_call(functools.partial(chain, members, atoms, own_rows, scale),...]
    all_gather x1 -> x0, waiting for transfers between devices: 138 us -> none  [shards(): return lax.all_gather(rebuilt, 'dp', axis=0, tiled=True)]
    dot_general x8 -> x0, matrix products: 31.3 us -> none  [the longest x1 19.3 us: shards(): lax.dot_general(hidden_act, out_grad, (((0,), (0,)), ((), ())), preferred...]
    unnamed x9 -> x4, local copies, waits for them, and re-layouts: 21.3 us -> 2.49 us
    another operation x10 -> x0, other arithmetic: 8.01 us -> none  [the longest x6 4.26 us: compress(): jnp.linalg.cholesky(gram_matrix + ridge_term * jnp.eye(atom_count, dtype=...]
  transfers between devices with their start and end apart: 2 -> 0, of which waited for: 2 -> 0; matrix products, arithmetic and copies ran while one was open for 0% -> 0% of each run, Pallas kernels for 0% -> 0%
where the time goes in v2:
time: 146 us
  Pallas kernels  143 us (98%)
  local copies, waits for them, and re-layouts  2.49 us (2%)
    pallas_call x1, Pallas kernels, shards(): pl.pallas_call(functools.partial(chain, members, atoms, own_rows, scale),...  129 us
    pallas_call x1, Pallas kernels, shards(): pl.pallas_call(rebuild_kernel, out_shape=jax.ShapeDtypeStruct((hidden_row...  13.7 us

profile of v2, /device:TPU:1, one launch (start us, length us, event | category | flops | bytes accessed | tf_op | source)
XLA Modules:
  0.0 146.3 jit_solution(9767816677339086657)
XLA Ops:
  0.7 0.0 copy-start
  0.7 1.5 %copy-done = bf16[256,3584]{1,0:T(8,128)(2,1)S(1)} copy-done((bf16[256,3584]{1,0:T(8,128)(2,1)S(1)}, bf16[256,3584]{1,0:T(8,128)(2,1)}, u32[]{:S(2)}) %copy-start) | copy-done | bytes 1835032
  2.2 0.0 copy-start.1
  2.2 1.0 copy-done.1
  3.1 129.5 %power_chain.1 = (bf16[4,4,4,2,16,768]{5,4,3,2,1,0:T(8,128)(2,1)S(1)}, bf16[16,2,16,256]{3,2,1,0:T(8,128)(2,1)S(1)}) custom-call(bf16[256,3584]{1,0:T(8,128)(2,1)S(1)} %copy-done, bf16[256,6144]{1,0:T(8,128)(2,1)} %o_hbm.1, f32[16,6144]{1,0:T(8,128)S(1)} %copy-done.1, s32[1,1]{1,0:T(1,128)} %bitcast.2.kept_ref), custom_call_target="tpu_custom_call" | custom-call | tf_op jit(solution)/shard_map/power_chain/pallas_call | solution.py:438
  132.6 13.7 %rebuild.1 = bf16[3584,3072]{1,0:T(8,128)(2,1)} custom-call(bf16[16,2,16,256]{3,2,1,0:T(8,128)(2,1)S(1)} %get-tuple-element.7.left_ref, bf16[4,16,2,16,768]{4,3,2,1,0:T(8,128)(2,1)S(1)} %bitcast.3), custom_call_target="tpu_custom_call" | custom-call | tf_op jit(solution)/shard_map/rebuild/pallas_call | solution.py:478
Async XLA Ops:
  0.7 1.5 %copy-start = (bf16[256,3584]{1,0:T(8,128)(2,1)S(1)}, bf16[256,3584]{1,0:T(8,128)(2,1)}, u32[]{:S(2)}) copy-start(bf16[256,3584]{1,0:T(8,128)(2,1)} %h_hbm.1) | copy-start | bytes 5505028
  2.2 1.0 copy-start.1

commit v3 on v0

v3 whole, which is shorter than its diff:
```python
import functools
import math

import jax
import jax.numpy as jnp
from jax import lax
from jax.experimental import pallas as pl
from jax.experimental.pallas import tpu as pltpu
from jax.sharding import PartitionSpec as P

POWER = 2
SIDE = 4
LANES = 128
GROUPS = 2
CHUNKS = 8
ROUNDS = (2, 2, 2, 2)
CUT = None
VMEM_BYTES = 60 * 1024 * 1024

F32 = jnp.float32
BF16 = jnp.bfloat16
NT = (((1,), (1,)), ((), ()))
TN = (((0,), (0,)), ((), ()))


def dot_nt(a, b):
    return lax.dot_general(a, b, NT, preferred_element_type=F32)


def dot_nn(a, b):
    return jnp.dot(a, b, preferred_element_type=F32)


def split2(x):
    high = x.astype(BF16)
    return jnp.concatenate([high, (x - high.astype(F32)).astype(BF16)], axis=0)


def split3(x):
    high = x.astype(BF16)
    rest = x - high.astype(F32)
    middle = rest.astype(BF16)
    low = (rest - middle.astype(F32)).astype(BF16)
    return jnp.concatenate([high, middle, low], axis=0)


def fold(x, times):
    rows = x.shape[0] // times
    total = x[:rows]
    for i in range(1, times):
        total = total + x[i * rows : (i + 1) * rows]
    return total


def orthonormal(left):
    atoms = left.shape[0]
    gram = lax.dot_general(left, left, NT, precision=lax.Precision.HIGHEST, preferred_element_type=F32)
    row = lax.broadcasted_iota(jnp.int32, (atoms, atoms), 0)
    col = lax.broadcasted_iota(jnp.int32, (atoms, atoms), 1)
    diagonal = row == col
    ridge = 1e-05 * jnp.sum(jnp.where(diagonal, gram, 0.0)) / atoms
    gram = gram + jnp.where(diagonal, ridge, 0.0)
    below = lax.broadcasted_iota(jnp.int32, (atoms, 1), 0)
    for j in range(atoms - 1):
        factor = jnp.where(below > j, gram[:, j : j + 1] / gram[j : j + 1, j : j + 1], 0.0)
        left = left - factor * left[j : j + 1]
        gram = gram - factor * gram[j : j + 1]
    pivots = jnp.sum(jnp.where(diagonal, gram, 0.0), axis=1, keepdims=True)
    return left / jnp.sqrt(pivots)


class Ring:
    def __init__(self, place, member):
        self.place, self.member = place, member

    def at(self, shift):
        return lax.rem(self.place + shift + SIDE, SIDE)

    def peer(self, shift):
        return self.member(self.at(shift))


SHIFTS = (1, 3, 2)


def chain(
    members,
    atoms,
    own_rows,
    scale,
    h_hbm,
    o_hbm,
    s_hbm,
    kept_ref,
    f2,
    left_out,
    h_v,
    o_v,
    s_v,
    hp,
    o_a,
    o_b,
    zs,
    zr,
    ls,
    lr,
    u_y,
    u_z,
    v_a,
    v_b,
    va_full,
    vb_full,
    w_a,
    w_b,
    rs_v,
    rs_w,
    f1,
    send_sems,
    recv_sems,
    local_sems,
):
    me = lax.axis_index("dp")
    pod = lax.axis_index("outer")
    y, z = lax.rem(me, SIDE), me // SIDE
    ring_y = Ring(y, lambda i: z * SIDE + i)
    ring_z = Ring(z, lambda i: i * SIDE + y)
    rows_ring = Ring(z + pod * (y - z), lambda i: (1 - pod) * (i * SIDE + y) + pod * (z * SIDE + i))
    cols_ring = Ring(y + pod * (z - y), lambda i: (1 - pod) * (z * SIDE + i) + pod * (i * SIDE + y))
    tokens, features = o_v.shape
    half = features // 2
    quarter = half // SIDE
    padded = hp.shape[2]
    share = members // GROUPS
    left_over = []
    taken = [0]

    def take(count):
        taken[0] += count
        return taken[0] - count

    def remote(src, dst, k, recv=None, **device):
        return pltpu.make_async_remote_copy(
            src_ref=src,
            dst_ref=dst,
            send_sem=send_sems.at[k],
            recv_sem=recv_sems.at[k if recv is None else recv],
            device_id=device,
            device_id_type=pl.DeviceIdType.MESH,
        )

    def send(src, dst, k, recv=None, **device):
        copy = remote(src, dst, k, recv, **device)
        copy.start()
        left_over.append(copy.wait_send)

    def came(dst, k, **device):
        remote(dst, dst, k, **device).wait_recv()

    def member(shift):
        return lax.rem(me + shift + members, members)

    load_o = pltpu.make_async_copy(o_hbm, o_v, local_sems.at[0])
    load_h = pltpu.make_async_copy(h_hbm, h_v, local_sems.at[1])
    load_s = pltpu.make_async_copy(s_hbm, s_v, local_sems.at[2])
    load_s.start()
    load_o.start()
    load_h.start()

    barrier = pltpu.get_barrier_semaphore()

    def greet(**device):
        pl.semaphore_signal(barrier, inc=1, device_id=device, device_id_type=pl.DeviceIdType.MESH)

    def greet_member(k, carry):
        greet(dp=member(k))
        return carry

    lax.fori_loop(1, members, greet_member, 0)
    greet(outer=1 - pod)
    for shift in SHIFTS:
        greet(dp=ring_y.peer(shift), outer=1 - pod)
        greet(dp=ring_z.peer(shift), outer=1 - pod)
    load_s.wait()
    start3 = split3(s_v[...])
    load_o.wait()
    pl.semaphore_wait(barrier, members + 2 * len(SHIFTS))

    regroup_base = take(2 * len(SHIFTS))
    plan = [
        (regroup_base + 2 * i + j, shift, ring, first, buf)
        for i, shift in enumerate(SHIFTS)
        for j, (ring, first, buf) in enumerate(((ring_y, 0, o_a), (ring_z, half, o_b)))
    ]
    rounds = [0]

    def regroup_rounds(count):
        rows = tokens // CHUNKS
        for r in range(rounds[0], min(rounds[0] + count, CHUNKS)):
            for k, shift, ring, first, buf in plan:
                begin = pl.multiple_of(first + ring.at(shift) * quarter, quarter)
                remote(
                    o_v.at[pl.ds(r * rows, rows), pl.ds(begin, quarter)],
                    buf.at[ring.place, pl.ds(r * rows, rows)],
                    k,
                    dp=ring.peer(shift),
                ).start()
        rounds[0] = min(rounds[0] + count, CHUNKS)

    def regroup_wait():
        if rounds[0] is None:
            return
        regroup_rounds(CHUNKS)
        rounds[0] = None
        for k, shift, ring, first, buf in plan:
            came(buf.at[ring.at(-shift)], k, dp=ring.peer(shift))
            left_over.append(
                remote(buf.at[ring.place], buf.at[ring.place], k, dp=ring.peer(shift)).wait_send
            )
        own_a.wait()
        own_b.wait()

    regroup_rounds(ROUNDS[0])
    own_a = pltpu.make_async_copy(
        o_v.at[:, pl.ds(pl.multiple_of(y * quarter, quarter), quarter)], o_a.at[y], local_sems.at[3]
    )
    own_b = pltpu.make_async_copy(
        o_v.at[:, pl.ds(pl.multiple_of(half + z * quarter, quarter), quarter)], o_b.at[z], local_sems.at[4]
    )
    own_a.start()
    own_b.start()

    first3 = split3(fold(dot_nt(start3, o_v[...]), 3))
    load_h.wait()

    def ring_gather(buf_of, ring):
        base = take(len(SHIFTS))
        own = buf_of(ring.place)
        for i, shift in enumerate(SHIFTS):
            send(own, own, base + i, dp=ring.peer(shift))

        def wait():
            for i, shift in enumerate(SHIFTS):
                came(buf_of(ring.at(-shift)), base + i, dp=ring.peer(shift))

        return wait

    def ring_sum(parts, land, ring):
        base = take(len(SHIFTS))
        for i, shift in enumerate(SHIFTS):
            send(parts.at[ring.at(shift)], land.at[i], base + i, dp=ring.peer(shift))

        def wait():
            for i, shift in enumerate(SHIFTS):
                came(land.at[i], base + i, dp=ring.peer(shift))

        def total():
            value = parts[ring.place].astype(F32)
            for i in range(len(SHIFTS)):
                value = value + land[i].astype(F32)
            return value

        return wait, total

    def both(*waits):
        def wait():
            for one in waits:
                one()

        return wait

    def piece_chain(g):
        owner = me // share == g
        first = g * share
        rows = slice(first * atoms, (first + share) * atoms)

        def fellow(k):
            return first + lax.rem(lax.rem(me, share) + k, share)

        def each_fellow(do):
            def loop(k, carry):
                do(k)
                return carry

            lax.fori_loop(1, share, loop, 0)
            pl.when(jnp.logical_not(owner))(lambda: do(0))

        def each_member(do):
            def loop(k, carry):
                do(k)
                return carry

            lax.fori_loop(1, members, loop, 0)

        for e in range(first, first + share):
            block = h_v[:, e * own_rows : (e + 1) * own_rows]
            hp[e] = jnp.concatenate([block, jnp.zeros((tokens, padded - own_rows), BF16)], axis=1)
            zs[0, e] = fold(dot_nn(first3, hp[e]), 3) * scale

        for step in range(POWER):
            last = step == POWER - 1
            z_base = take(members)

            def z_copy(k, step=step, z_base=z_base):
                to = fellow(k)
                return remote(zs.at[step, to], zr.at[step, me], z_base + k, z_base + me, dp=to)

            each_fellow(lambda k: z_copy(k).start())
            left_over.append(lambda z_copy=z_copy: each_fellow(lambda k: z_copy(k).wait_send()))

            def z_wait():
                def arrive(k):
                    source = member(k)
                    came(zr.at[step, source], z_base + source, dp=source)

                pl.when(owner)(lambda: each_member(arrive))

            yield z_wait

            left_base = take(members)

            def left_copy(k, step=step, left_base=left_base):
                to = member(k)
                return remote(
                    ls.at[step], lr.at[step, me], left_base + k, left_base + lax.rem(me, share), dp=to
                )

            @pl.when(owner)
            def _():
                zr[step, me] = zs[step, me]
                left = orthonormal(jnp.sum(zr[step], axis=0))
                if last:
                    atom = lax.broadcasted_iota(jnp.int32, (atoms, 1), 0)
                    left = jnp.where(atom < kept_ref[0, 0], left, 0.0)
                pair = split2(left)
                ls[step] = pair
                lr[step, me] = pair
                each_member(lambda k: left_copy(k).start())

            def left_sent(left_copy=left_copy):
                pl.when(owner)(lambda: each_member(lambda k: left_copy(k).wait_send()))

            left_over.append(left_sent)

            def left_wait():
                def arrive(k):
                    source = fellow(k)
                    came(lr.at[step, source], left_base + lax.rem(source, share), dp=source)

                each_fellow(arrive)

            yield left_wait

            for e in range(first, first + share):
                block = (fold(dot_nt(lr[step, e], hp[e]), 2) * scale).astype(BF16)
                u_y[step, y, e * atoms : (e + 1) * atoms] = block
                u_z[step, z, e * atoms : (e + 1) * atoms] = block
            group_rows = pl.ds(first * atoms, share * atoms)
            waits = both(
                ring_gather(lambda i: u_y.at[step, i, group_rows], ring_y),
                ring_gather(lambda i: u_z.at[step, i, group_rows], ring_z),
            )
            if last:
                own_left = pltpu.make_async_copy(
                    lr.at[step, pl.ds(first, share), pl.ds(0, atoms)],
                    left_out.at[pl.ds(first, share), pod],
                    local_sems.at[5 + g],
                )
                own_left.start()
                left_over.append(own_left.wait)
                k = take(1)
                send(
                    lr.at[step, pl.ds(first, share), pl.ds(0, atoms)],
                    left_out.at[pl.ds(first, share), pod],
                    k,
                    outer=1 - pod,
                )
                other_left = left_out.at[pl.ds(first, share), 1 - pod]
                left_over.append(lambda k=k, ref=other_left: came(ref, k, outer=1 - pod))
            yield waits

            regroup_wait()
            for u, o, v in ((u_y, o_a, v_a), (u_z, o_b, v_b)):
                total = dot_nn(u[step, 0, rows], o[0])
                for c in range(1, SIDE):
                    total = total + dot_nn(u[step, c, rows], o[c])
                v[step, g] = total.astype(BF16).reshape(v.shape[2:])
            wait_a, total_a = ring_sum(v_a.at[step, g], rs_v.at[step, g, 0], ring_z)
            wait_b, total_b = ring_sum(v_b.at[step, g], rs_v.at[step, g, 1], ring_y)
            yield both(wait_a, wait_b)
            if last:
                break
            va_full[g, z] = total_a().astype(BF16)
            vb_full[g, y] = total_b().astype(BF16)
            yield both(
                ring_gather(lambda i: va_full.at[g, i], ring_z),
                ring_gather(lambda i: vb_full.at[g, i], ring_y),
            )
            for v, o, w in ((va_full, o_a, w_a), (vb_full, o_b, w_b)):
                whole = v[g].reshape(share * atoms, quarter)
                for c in range(SIDE):
                    w[g, c] = dot_nt(whole, o[c]).astype(BF16)
            wait_a, total_a = ring_sum(w_a.at[g], rs_w.at[g, 0], ring_y)
            wait_b, total_b = ring_sum(w_b.at[g], rs_w.at[g, 1], ring_z)
            yield both(wait_a, wait_b)
            token_side = total_a() + total_b()
            for i in range(share):
                pair = split2(token_side[i * atoms : (i + 1) * atoms])
                zs[step + 1, first + i] = fold(dot_nn(pair, hp[first + i]), 2) * scale

        per_row = share // SIDE
        f1[g, 0] = total_a().astype(BF16).reshape(per_row, atoms, quarter)
        f1[g, 1] = total_b().astype(BF16).reshape(per_row, atoms, quarter)
        row, col = rows_ring.place, cols_ring.place
        base = take(7)
        for i, shift in enumerate(SHIFTS):
            at = base + 2 * i + pod
            send(f1.at[g, 0], f2.at[y, g, z, :, pod], base + i, at, dp=ring_z.peer(shift), outer=0)
            send(f1.at[g, 1], f2.at[z, g, y, :, pod], base + 3 + i, at, dp=ring_y.peer(shift), outer=1)
        send(f1.at[g, 1 - pod], f2.at[row, g, col, :, pod], base + 6, outer=1 - pod)
        keep = pltpu.make_async_copy(f1.at[g, pod], f2.at[col, g, row, :, pod], local_sems.at[5 + GROUPS + g])
        keep.start()

        def own_wait():
            keep.wait()
            came(f2.at[col, g, row, :, 1 - pod], base + 6, outer=1 - pod)

        yield own_wait

        units = []

        def unit_start(slot):
            k = take(6)

            def ref(place, which):
                return f2.at[place, g, slot, :, which]

            def go(shift, which, to, i):
                r = ref(cols_ring.at(shift), which)
                send(r, r, k + i, dp=cols_ring.peer(to))

            def arrived(shift, which, i):
                came(ref(cols_ring.at(shift), which), k + i, dp=cols_ring.peer(1))

            go(0, 0, 1, 0)
            go(0, 1, -1, 2)
            go(0, 1, 1, 1)
            go(0, 0, -1, 3)

            def forward():
                arrived(-1, 0, 0)
                go(-1, 0, 1, 4)
                arrived(1, 1, 2)
                go(1, 1, -1, 5)

            def finish():
                arrived(-1, 1, 1)
                arrived(1, 0, 3)
                arrived(2, 0, 4)
                arrived(2, 1, 5)

            units.append((forward, finish))

        unit_start(row)
        for i, shift in enumerate(SHIFTS):
            slot = rows_ring.at(-shift)

            def row_wait():
                for q in range(2):
                    came(f2.at[col, g, slot, :, q], base + 2 * i + q, dp=rows_ring.peer(shift))

            yield row_wait
            unit_start(slot)
            units[i][0]()
        yield units[-1][0]
        for forward, finish in units:
            finish()

    chains = [piece_chain(g) for g in range(GROUPS)]
    waits = [lambda: None] * GROUPS
    cycle = 0
    while any(wait is not None for wait in waits):
        for g in range(GROUPS):
            if waits[g] is not None:
                waits[g]()
                waits[g] = next(chains[g], None)
        cycle += 1
        if cycle < len(ROUNDS):
            regroup_rounds(ROUNDS[cycle])
        if cycle == CUT:
            for wait in waits:
                wait()
            regroup_wait()
            break
    for wait in left_over:
        wait()


def rebuild_kernel(left_hbm, right_hbm, out_hbm, left_v, right_v, out_v, sems):
    pieces, own_rows, _ = out_v.shape
    width = right_v.shape[-1]
    load_left = pltpu.make_async_copy(left_hbm, left_v, sems.at[2 * pieces])
    load_left.start()
    loads = [pltpu.make_async_copy(right_hbm.at[:, e], right_v.at[:, e], sems.at[e]) for e in range(pieces)]
    stores = [
        pltpu.make_async_copy(out_v.at[e], out_hbm.at[pl.ds(e * own_rows, own_rows)], sems.at[pieces + e])
        for e in range(pieces)
    ]
    for load in loads:
        load.start()
    load_left.wait()
    for e in range(pieces):
        left = left_v[e].reshape(-1, left_v.shape[-1])[:, :own_rows]
        loads[e].wait()
        for c in range(SIDE):
            right = right_v[c, e].reshape(left.shape[0], width)
            out_v[e, :, c * width : (c + 1) * width] = lax.dot_general(
                left, right, TN, preferred_element_type=F32
            ).astype(BF16)
        stores[e].start()
    for store in stores:
        store.wait()


def shards(hidden_act, out_grad, start_vectors, kept_counts):
    tokens, features = out_grad.shape
    atoms = start_vectors.shape[0]
    members = lax.axis_size("dp")
    pods = lax.axis_size("outer")
    hidden_rows = hidden_act.shape[1]
    own_rows = hidden_rows // members
    padded = -(-own_rows // LANES) * LANES
    quarter = features // 2 // SIDE
    share = members // GROUPS
    part = share * atoms // SIDE
    per_row = share // SIDE
    scale = 1.0 / math.sqrt(tokens * members)
    any_space = pl.BlockSpec(memory_space=pl.ANY)
    sem_count = 6 + GROUPS * (POWER * (2 * members + 12) + 12 + 1 + 7 + 24)
    right_atoms, left_atoms = pl.pallas_call(
        functools.partial(chain, members, atoms, own_rows, scale),
        out_shape=(
            jax.ShapeDtypeStruct((SIDE, GROUPS, SIDE, per_row, pods, atoms, quarter), BF16),
            jax.ShapeDtypeStruct((members, pods, atoms, padded), BF16),
        ),
        in_specs=[any_space, any_space, any_space, pl.BlockSpec(memory_space=pltpu.SMEM)],
        out_specs=(any_space, any_space),
        scratch_shapes=[
            pltpu.VMEM((tokens, hidden_rows), BF16),
            pltpu.VMEM((tokens, features), BF16),
            pltpu.VMEM((atoms, features), F32),
            pltpu.VMEM((members, tokens, padded), BF16),
            pltpu.VMEM((SIDE, tokens, quarter), BF16),
            pltpu.VMEM((SIDE, tokens, quarter), BF16),
            pltpu.VMEM((POWER, members, atoms, padded), F32),
            pltpu.VMEM((POWER, members, atoms, padded), F32),
            pltpu.VMEM((POWER, 2 * atoms, padded), BF16),
            pltpu.VMEM((POWER, members, 2 * atoms, padded), BF16),
            pltpu.VMEM((POWER, SIDE, members * atoms, tokens), BF16),
            pltpu.VMEM((POWER, SIDE, members * atoms, tokens), BF16),
            pltpu.VMEM((POWER, GROUPS, SIDE, part, quarter), BF16),
            pltpu.VMEM((POWER, GROUPS, SIDE, part, quarter), BF16),
            pltpu.VMEM((GROUPS, SIDE, part, quarter), BF16),
            pltpu.VMEM((GROUPS, SIDE, part, quarter), BF16),
            pltpu.VMEM((GROUPS, SIDE, share * atoms, tokens), BF16),
            pltpu.VMEM((GROUPS, SIDE, share * atoms, tokens), BF16),
            pltpu.VMEM((POWER, GROUPS, 2, 3, part, quarter), BF16),
            pltpu.VMEM((GROUPS, 2, 3, share * atoms, tokens), BF16),
            pltpu.VMEM((GROUPS, 2, per_row, atoms, quarter), BF16),
            pltpu.SemaphoreType.DMA((sem_count,)),
            pltpu.SemaphoreType.DMA((sem_count,)),
            pltpu.SemaphoreType.DMA((5 + 2 * GROUPS,)),
        ],
        compiler_params=pltpu.CompilerParams(
            collective_id=0, has_side_effects=True, vmem_limit_bytes=VMEM_BYTES
        ),
        name="power_chain",
    )(hidden_act, out_grad, start_vectors, kept_counts.reshape(1, 1))
    return pl.pallas_call(
        rebuild_kernel,
        out_shape=jax.ShapeDtypeStruct((hidden_rows, features // pods), BF16),
        in_specs=[any_space, any_space],
        out_specs=any_space,
        scratch_shapes=[
            pltpu.VMEM((members, pods, atoms, padded), BF16),
            pltpu.VMEM((SIDE, members, pods, atoms, quarter), BF16),
            pltpu.VMEM((members, own_rows, features // pods), BF16),
            pltpu.SemaphoreType.DMA((2 * members + 1,)),
        ],
        compiler_params=pltpu.CompilerParams(vmem_limit_bytes=VMEM_BYTES),
        name="rebuild",
    )(left_atoms, right_atoms.reshape(SIDE, members, pods, atoms, quarter))


def solution(mesh):
    placed = (
        P(("dp", "outer"), "tensor"),
        P(("dp", "outer"), None),
        P(),
        P("tensor", "outer", "dp"),
    )
    return jax.shard_map(
        shards, mesh=mesh, in_specs=placed, out_specs=P("tensor", "outer"), check_vma=False
    )
```

time: 469 us -> 121 us (0.26)
  waiting for transfers between devices: 388 us -> 0 us
  Pallas kernels: 0 us -> 118 us
  matrix products: 31.7 us -> 0 us
  local copies, waits for them, and re-layouts: 21.4 us -> 0 us
  between operations: 15.5 us -> 0.82 us
  other arithmetic: 8.05 us -> 0 us
    reduce_scatter x1 -> x0, waiting for transfers between devices: 250 us -> none  [shards(): lax.psum_scatter((lax.dot_general(hidden_act, out_grad, (((0,), (0,)), ((...]
    all_gather x1 -> x0, waiting for transfers between devices: 138 us -> none  [shards(): return lax.all_gather(rebuilt, 'dp', axis=0, tiled=True)]
    pallas_call x0 -> x2, Pallas kernels: none -> 118 us  [the longest x1 107 us: shards(): pl.pallas_call(functools.partial(chain, members, atoms, own_rows, scale),...]
    dot_general x8 -> x0, matrix products: 31.3 us -> none  [the longest x1 19.3 us: shards(): lax.dot_general(hidden_act, out_grad, (((0,), (0,)), ((), ())), preferred...]
    unnamed x9 -> x0, local copies, waits for them, and re-layouts: 21.3 us -> none
    another operation x10 -> x0, other arithmetic: 8.01 us -> none  [the longest x6 4.26 us: compress(): jnp.linalg.cholesky(gram_matrix + ridge_term * jnp.eye(atom_count, dtype=...]
  transfers between devices with their start and end apart: 2 -> 0, of which waited for: 2 -> 0; matrix products, arithmetic and copies ran while one was open for 0% -> 0% of each run, Pallas kernels for 0% -> 0%
where the time goes in v3:
time: 121 us; the launch traced here: 119 us
  Pallas kernels  118 us (98%)
    pallas_call x1, Pallas kernels, shards(): pl.pallas_call(functools.partial(chain, members, atoms, own_rows, scale),...  107 us
    pallas_call x1, Pallas kernels, shards(): pl.pallas_call(rebuild_kernel, out_shape=jax.ShapeDtypeStruct((hidden_row...  11 us

profile of v3, /device:TPU:1, one launch (start us, length us, event | category | flops | bytes accessed | tf_op | source)
XLA Modules:
  0.0 119.2 jit_solution(3056654741921426283)
XLA Ops:
  0.7 107.4 %power_chain.1 = (bf16[4,2,4,2,2,16,768]{6,5,4,3,2,1,0:T(8,128)(2,1)}, bf16[16,2,16,256]{3,2,1,0:T(8,128)(2,1)}) custom-call(bf16[256,3584]{1,0:T(8,128)(2,1)} %h_hbm.1, bf16[256,6144]{1,0:T(8,128)(2,1)} %o_hbm.1, f32[16,6144]{1,0:T(8,128)} %s_hbm.1, s32[1,1]{1,0:T(1,128)} %bitcast.2.kept_ref), custom_call_target="tpu_custom_call" | custom-call | tf_op jit(solution)/shard_map/power_chain/pallas_call | solution.py:539
  108.0 11.0 %rebuild.1 = bf16[3584,3072]{1,0:T(8,128)(2,1)} custom-call(bf16[16,2,16,256]{3,2,1,0:T(8,128)(2,1)} %get-tuple-element.7.left_hbm, bf16[4,16,2,16,768]{4,3,2,1,0:T(8,128)(2,1)} %bitcast.3), custom_call_target="tpu_custom_call" | custom-call | tf_op jit(solution)/shard_map/rebuild/pallas_call | solution.py:578

commit v4 on v3

--- a/solution.py
+++ b/solution.py
@@ -12,8 +12,8 @@
 SIDE = 4
 LANES = 128
 GROUPS = 2
-CHUNKS = 8
-ROUNDS = (2, 2, 2, 2)
+CHUNKS = 4
+ROUNDS = (1, 1, 1, 1)
 CUT = None
 VMEM_BYTES = 60 * 1024 * 1024
 
@@ -92,7 +92,7 @@
     o_hbm,
     s_hbm,
     kept_ref,
-    f2,
+    right_out,
     left_out,
     h_v,
     o_v,
@@ -115,6 +115,7 @@
     rs_v,
     rs_w,
     f1,
+    f2,
     send_sems,
     recv_sems,
     local_sems,
@@ -149,12 +150,13 @@
         )
 
     def send(src, dst, k, recv=None, **device):
-        copy = remote(src, dst, k, recv, **device)
-        copy.start()
-        left_over.append(copy.wait_send)
-
-    def came(dst, k, **device):
-        remote(dst, dst, k, **device).wait_recv()
+        remote(src, dst, k, recv, **device).start()
+
+    def came(dst, k):
+        remote(dst, dst, k, outer=1 - pod).wait_recv()
+
+    def went(src, k):
+        left_over.append(lambda: remote(src, src, k, outer=1 - pod).wait_send())
 
     def member(shift):
         return lax.rem(me + shift + members, members)
@@ -212,10 +214,8 @@
         regroup_rounds(CHUNKS)
         rounds[0] = None
         for k, shift, ring, first, buf in plan:
-            came(buf.at[ring.at(-shift)], k, dp=ring.peer(shift))
-            left_over.append(
-                remote(buf.at[ring.place], buf.at[ring.place], k, dp=ring.peer(shift)).wait_send
-            )
+            came(buf.at[ring.at(-shift)], k)
+            went(buf.at[ring.place], k)
         own_a.wait()
         own_b.wait()
 
@@ -232,26 +232,23 @@
     first3 = split3(fold(dot_nt(start3, o_v[...]), 3))
     load_h.wait()
 
-    def ring_gather(buf_of, ring):
-        base = take(len(SHIFTS))
-        own = buf_of(ring.place)
+    def ring_gather(buf, ring):
+        k = take(1)
+        own = buf(ring.place)
+        for shift in SHIFTS:
+            send(own, own, k, dp=ring.peer(shift))
+        three = buf(pl.ds(0, len(SHIFTS)))
+        went(three, k)
+        return lambda: came(three, k)
+
+    def ring_sum(parts, land, ring):
+        k = take(1)
         for i, shift in enumerate(SHIFTS):
-            send(own, own, base + i, dp=ring.peer(shift))
+            send(parts.at[ring.at(shift)], land.at[i], k, dp=ring.peer(shift))
+        went(land, k)
 
         def wait():
-            for i, shift in enumerate(SHIFTS):
-                came(buf_of(ring.at(-shift)), base + i, dp=ring.peer(shift))
-
-        return wait
-
-    def ring_sum(parts, land, ring):
-        base = take(len(SHIFTS))
-        for i, shift in enumerate(SHIFTS):
-            send(parts.at[ring.at(shift)], land.at[i], base + i, dp=ring.peer(shift))
-
-        def wait():
-            for i, shift in enumerate(SHIFTS):
-                came(land.at[i], base + i, dp=ring.peer(shift))
+            came(land, k)
 
         def total():
             value = parts[ring.place].astype(F32)
@@ -284,6 +281,10 @@
             lax.fori_loop(1, share, loop, 0)
             pl.when(jnp.logical_not(owner))(lambda: do(0))
 
+        def by_owner(wait, call=lambda f: f()):
+            call(lambda: pl.when(owner)(lambda: wait(share - 1)))
+            call(lambda: pl.when(jnp.logical_not(owner))(lambda: wait(share)))
+
         def each_member(do):
             def loop(k, carry):
                 do(k)
@@ -294,64 +295,60 @@
         for e in range(first, first + share):
             block = h_v[:, e * own_rows : (e + 1) * own_rows]
             hp[e] = jnp.concatenate([block, jnp.zeros((tokens, padded - own_rows), BF16)], axis=1)
-            zs[0, e] = fold(dot_nn(first3, hp[e]), 3) * scale
+            zs[0, e] = (fold(dot_nn(first3, hp[e]), 3) * scale).astype(BF16)
 
         for step in range(POWER):
             last = step == POWER - 1
-            z_base = take(members)
-
-            def z_copy(k, step=step, z_base=z_base):
+            z_k = take(1)
+
+            def z_send(k):
                 to = fellow(k)
-                return remote(zs.at[step, to], zr.at[step, me], z_base + k, z_base + me, dp=to)
-
-            each_fellow(lambda k: z_copy(k).start())
-            left_over.append(lambda z_copy=z_copy: each_fellow(lambda k: z_copy(k).wait_send()))
+                send(zs.at[step, to], zr.at[step, me], z_k, dp=to)
+
+            each_fellow(z_send)
+            by_owner(
+                lambda count, step=step, z_k=z_k: remote(
+                    zs.at[step, pl.ds(0, count)], zs.at[step, pl.ds(0, count)], z_k, outer=1 - pod
+                ).wait_send(),
+                left_over.append,
+            )
 
             def z_wait():
-                def arrive(k):
-                    source = member(k)
-                    came(zr.at[step, source], z_base + source, dp=source)
-
-                pl.when(owner)(lambda: each_member(arrive))
+                pl.when(owner)(lambda: came(zr.at[step, pl.ds(0, members - 1)], z_k))
 
             yield z_wait
 
-            left_base = take(members)
-
-            def left_copy(k, step=step, left_base=left_base):
-                to = member(k)
-                return remote(
-                    ls.at[step], lr.at[step, me], left_base + k, left_base + lax.rem(me, share), dp=to
-                )
+            left_k = take(2)
 
             @pl.when(owner)
             def _():
                 zr[step, me] = zs[step, me]
-                left = orthonormal(jnp.sum(zr[step], axis=0))
+                left = orthonormal(jnp.sum(zr[step].astype(F32), axis=0))
                 if last:
                     atom = lax.broadcasted_iota(jnp.int32, (atoms, 1), 0)
                     left = jnp.where(atom < kept_ref[0, 0], left, 0.0)
-                pair = split2(left)
-                ls[step] = pair
-                lr[step, me] = pair
-                each_member(lambda k: left_copy(k).start())
-
-            def left_sent(left_copy=left_copy):
-                pl.when(owner)(lambda: each_member(lambda k: left_copy(k).wait_send()))
+                rounded = left.astype(BF16)
+                ls[step] = rounded
+                lr[step, me] = rounded
+
+                def left_send(k):
+                    send(ls.at[step], lr.at[step, me], left_k, left_k + 1, dp=member(k))
+
+                each_member(left_send)
+
+            def left_sent(step=step, left_k=left_k):
+                all_sent = lr.at[step, pl.ds(0, members - 1)]
+                pl.when(owner)(lambda: remote(all_sent, all_sent, left_k, outer=1 - pod).wait_send())
 
             left_over.append(left_sent)
 
             def left_wait():
-                def arrive(k):
-                    source = fellow(k)
-                    came(lr.at[step, source], left_base + lax.rem(source, share), dp=source)
-
-                each_fellow(arrive)
+                by_owner(lambda count: came(lr.at[step, pl.ds(first, count)], left_k + 1))
 
             yield left_wait
 
             for e in range(first, first + share):
-                block = (fold(dot_nt(lr[step, e], hp[e]), 2) * scale).astype(BF16)
+                block = (dot_nt(lr[step, e], hp[e]) * scale).astype(BF16)
                 u_y[step, y, e * atoms : (e + 1) * atoms] = block
                 u_z[step, z, e * atoms : (e + 1) * atoms] = block
             group_rows = pl.ds(first * atoms, share * atoms)
@@ -361,7 +358,7 @@
             )
             if last:
                 own_left = pltpu.make_async_copy(
-                    lr.at[step, pl.ds(first, share), pl.ds(0, atoms)],
+                    lr.at[step, pl.ds(first, share)],
                     left_out.at[pl.ds(first, share), pod],
                     local_sems.at[5 + g],
                 )
@@ -369,13 +366,14 @@
                 left_over.append(own_left.wait)
                 k = take(1)
                 send(
-                    lr.at[step, pl.ds(first, share), pl.ds(0, atoms)],
+                    lr.at[step, pl.ds(first, share)],
                     left_out.at[pl.ds(first, share), pod],
                     k,
                     outer=1 - pod,
                 )
                 other_left = left_out.at[pl.ds(first, share), 1 - pod]
-                left_over.append(lambda k=k, ref=other_left: came(ref, k, outer=1 - pod))
+                went(other_left, k)
+                left_over.append(lambda k=k, ref=other_left: came(ref, k))
             yield waits
 
             regroup_wait()
@@ -405,75 +403,18 @@
             token_side = total_a() + total_b()
             for i in range(share):
                 pair = split2(token_side[i * atoms : (i + 1) * atoms])
-                zs[step + 1, first + i] = fold(dot_nn(pair, hp[first + i]), 2) * scale
-
-        per_row = share // SIDE
-        f1[g, 0] = total_a().astype(BF16).reshape(per_row, atoms, quarter)
-        f1[g, 1] = total_b().astype(BF16).reshape(per_row, atoms, quarter)
-        row, col = rows_ring.place, cols_ring.place
-        base = take(7)
+                zs[step + 1, first + i] = (fold(dot_nn(pair, hp[first + i]), 2) * scale).astype(BF16)
+
+        f1[g, 0] = total_a().astype(BF16).reshape(f1.shape[2:])
+        f1[g, 1] = total_b().astype(BF16).reshape(f1.shape[2:])
         for i, shift in enumerate(SHIFTS):
-            at = base + 2 * i + pod
-            send(f1.at[g, 0], f2.at[y, g, z, :, pod], base + i, at, dp=ring_z.peer(shift), outer=0)
-            send(f1.at[g, 1], f2.at[z, g, y, :, pod], base + 3 + i, at, dp=ring_y.peer(shift), outer=1)
-        send(f1.at[g, 1 - pod], f2.at[row, g, col, :, pod], base + 6, outer=1 - pod)
-        keep = pltpu.make_async_copy(f1.at[g, pod], f2.at[col, g, row, :, pod], local_sems.at[5 + GROUPS + g])
-        keep.start()
-
-        def own_wait():
-            keep.wait()
-            came(f2.at[col, g, row, :, 1 - pod], base + 6, outer=1 - pod)
-
-        yield own_wait
-
-        units = []
-
-        def unit_start(slot):
-            k = take(6)
-
-            def ref(place, which):
-                return f2.at[place, g, slot, :, which]
-
-            def go(shift, which, to, i):
-                r = ref(cols_ring.at(shift), which)
-                send(r, r, k + i, dp=cols_ring.peer(to))
-
-            def arrived(shift, which, i):
-                came(ref(cols_ring.at(shift), which), k + i, dp=cols_ring.peer(1))
-
-            go(0, 0, 1, 0)
-            go(0, 1, -1, 2)
-            go(0, 1, 1, 1)
-            go(0, 0, -1, 3)
-
-            def forward():
-                arrived(-1, 0, 0)
-                go(-1, 0, 1, 4)
-                arrived(1, 1, 2)
-                go(1, 1, -1, 5)
-
-            def finish():
-                arrived(-1, 1, 1)
-                arrived(1, 0, 3)
-                arrived(2, 0, 4)
-                arrived(2, 1, 5)
-
-            units.append((forward, finish))
-
-        unit_start(row)
-        for i, shift in enumerate(SHIFTS):
-            slot = rows_ring.at(-shift)
-
-            def row_wait():
-                for q in range(2):
-                    came(f2.at[col, g, slot, :, q], base + 2 * i + q, dp=rows_ring.peer(shift))
-
-            yield row_wait
-            unit_start(slot)
-            units[i][0]()
-        yield units[-1][0]
-        for forward, finish in units:
-            finish()
+            send(f1.at[g, 0], f2.at[y, z, g, :, pod], row_k, row_k + i, dp=ring_z.peer(shift), outer=0)
+            send(f1.at[g, 1], f2.at[z, y, g, :, pod], row_k, row_k + i, dp=ring_y.peer(shift), outer=1)
+        send(f1.at[g, 1 - pod], f2.at[row, col, g, :, pod], cross_k, outer=1 - pod)
+        f2[col, row, g, :, pod] = f1[g, pod]
+
+    row, col = rows_ring.place, cols_ring.place
+    row_k, cross_k, unit_k, far_k = take(len(SHIFTS)), take(1), take(2 * SIDE), take(1)
 
     chains = [piece_chain(g) for g in range(GROUPS)]
     waits = [lambda: None] * GROUPS
@@ -488,19 +429,60 @@
             regroup_rounds(ROUNDS[cycle])
         if cycle == CUT:
             for wait in waits:
-                wait()
+                if wait is not None:
+                    wait()
             regroup_wait()
             break
+    if CUT is None:
+        went(f2.at[0, pl.ds(0, 3)], row_k)
+
+        def go(shift, slot, which, to, recv):
+            ref = f2.at[cols_ring.at(shift), slot, :, :, which]
+            send(ref, ref, far_k, recv, dp=cols_ring.peer(to))
+
+        def unit_start(slot, i):
+            go(0, slot, 0, 1, unit_k + 2 * i)
+            go(0, slot, 1, -1, unit_k + 2 * i + 1)
+            go(0, slot, 1, 1, far_k)
+            go(0, slot, 0, -1, far_k)
+
+        def unit_forward(slot, i):
+            came(f2.at[cols_ring.at(-1), slot, :, :, 0], unit_k + 2 * i)
+            go(-1, slot, 0, 1, far_k)
+            came(f2.at[cols_ring.at(1), slot, :, :, 1], unit_k + 2 * i + 1)
+            go(1, slot, 1, -1, far_k)
+
+        came(f2.at[col, row, :, :, 1 - pod], cross_k)
+        went(f2.at[col, row, :, :, 1 - pod], cross_k)
+        unit_start(row, 0)
+        slots = [row]
+        for i, shift in enumerate(SHIFTS):
+            slots.append(rows_ring.at(-shift))
+            came(f2.at[col, slots[-1]], row_k + i)
+            unit_start(slots[-1], i + 1)
+            unit_forward(slots[-2], i)
+        unit_forward(slots[-1], SIDE - 1)
+        came(f2.at[pl.ds(0, 2)], far_k)
+        went(f2.at[pl.ds(0, 3)], far_k)
+        out = pltpu.make_async_copy(f2, right_out, local_sems.at[5 + GROUPS])
+        out.start()
+        left_over.append(out.wait)
     for wait in left_over:
         wait()
 
 
 def rebuild_kernel(left_hbm, right_hbm, out_hbm, left_v, right_v, out_v, sems):
     pieces, own_rows, _ = out_v.shape
+    per_row = pieces // GROUPS // SIDE
+
+    def place(e):
+        group, rest = divmod(e, pieces // GROUPS)
+        return rest // per_row * (pieces // SIDE) + group * per_row + rest % per_row
+
     width = right_v.shape[-1]
     load_left = pltpu.make_async_copy(left_hbm, left_v, sems.at[2 * pieces])
     load_left.start()
-    loads = [pltpu.make_async_copy(right_hbm.at[:, e], right_v.at[:, e], sems.at[e]) for e in range(pieces)]
+    loads = [pltpu.make_async_copy(right_hbm.at[:, place(e)], right_v.at[:, e], sems.at[e]) for e in range(pieces)]
     stores = [
         pltpu.make_async_copy(out_v.at[e], out_hbm.at[pl.ds(e * own_rows, own_rows)], sems.at[pieces + e])
         for e in range(pieces)
@@ -535,11 +517,11 @@
     per_row = share // SIDE
     scale = 1.0 / math.sqrt(tokens * members)
     any_space = pl.BlockSpec(memory_space=pl.ANY)
-    sem_count = 6 + GROUPS * (POWER * (2 * members + 12) + 12 + 1 + 7 + 24)
+    sem_count = 6 + GROUPS * (POWER * 7 + 5) + 13
     right_atoms, left_atoms = pl.pallas_call(
         functools.partial(chain, members, atoms, own_rows, scale),
         out_shape=(
-            jax.ShapeDtypeStruct((SIDE, GROUPS, SIDE, per_row, pods, atoms, quarter), BF16),
+            jax.ShapeDtypeStruct((SIDE, SIDE, GROUPS, per_row, pods, atoms, quarter), BF16),
             jax.ShapeDtypeStruct((members, pods, atoms, padded), BF16),
         ),
         in_specs=[any_space, any_space, any_space, pl.BlockSpec(memory_space=pltpu.SMEM)],
@@ -551,10 +533,10 @@
             pltpu.VMEM((members, tokens, padded), BF16),
             pltpu.VMEM((SIDE, tokens, quarter), BF16),
             pltpu.VMEM((SIDE, tokens, quarter), BF16),
-            pltpu.VMEM((POWER, members, atoms, padded), F32),
-            pltpu.VMEM((POWER, members, atoms, padded), F32),
-            pltpu.VMEM((POWER, 2 * atoms, padded), BF16),
-            pltpu.VMEM((POWER, members, 2 * atoms, padded), BF16),
+            pltpu.VMEM((POWER, members, atoms, padded), BF16),
+            pltpu.VMEM((POWER, members, atoms, padded), BF16),
+            pltpu.VMEM((POWER, atoms, padded), BF16),
+            pltpu.VMEM((POWER, members, atoms, padded), BF16),
             pltpu.VMEM((POWER, SIDE, members * atoms, tokens), BF16),
             pltpu.VMEM((POWER, SIDE, members * atoms, tokens), BF16),
             pltpu.VMEM((POWER, GROUPS, SIDE, part, quarter), BF16),
@@ -566,9 +548,10 @@
             pltpu.VMEM((POWER, GROUPS, 2, 3, part, quarter), BF16),
             pltpu.VMEM((GROUPS, 2, 3, share * atoms, tokens), BF16),
             pltpu.VMEM((GROUPS, 2, per_row, atoms, quarter), BF16),
+            pltpu.VMEM((SIDE, SIDE, GROUPS, per_row, pods, atoms, quarter), BF16),
             pltpu.SemaphoreType.DMA((sem_count,)),
             pltpu.SemaphoreType.DMA((sem_count,)),
-            pltpu.SemaphoreType.DMA((5 + 2 * GROUPS,)),
+            pltpu.SemaphoreType.DMA((6 + GROUPS,)),
         ],
         compiler_params=pltpu.CompilerParams(
             collective_id=0, has_side_effects=True, vmem_limit_bytes=VMEM_BYTES

time: 121 us -> 109 us (0.901); the launches traced: 119 us -> 109 us
  Pallas kernels: 118 us -> 108 us
    pallas_call x1, Pallas kernels: 107 us -> 97 us  [shards(): pl.pallas_call(functools.partial(chain, members, atoms, own_rows, scale),...]
where the time goes in v4:
time: 109 us
  Pallas kernels  108 us (99%)
    pallas_call x1, Pallas kernels, shards(): pl.pallas_call(functools.partial(chain, members, atoms, own_rows, scale),...  97 us
    pallas_call x1, Pallas kernels, shards(): pl.pallas_call(rebuild_kernel, out_shape=jax.ShapeDtypeStruct((hidden_row...  11 us

profile of v4, /device:TPU:1, one launch (start us, length us, event | category | flops | bytes accessed | tf_op | source)
XLA Modules:
  0.0 108.9 jit_solution(4863032587954114206)
XLA Ops:
  0.7 97.0 %power_chain.1 = (bf16[4,4,2,2,2,16,768]{6,5,4,3,2,1,0:T(8,128)(2,1)}, bf16[16,2,16,256]{3,2,1,0:T(8,128)(2,1)}) custom-call(bf16[256,3584]{1,0:T(8,128)(2,1)} %h_hbm.1, bf16[256,6144]{1,0:T(8,128)(2,1)} %o_hbm.1, f32[16,6144]{1,0:T(8,128)} %s_hbm.1, s32[1,1]{1,0:T(1,128)} %bitcast.2.kept_ref), custom_call_target="tpu_custom_call" | custom-call | tf_op jit(solution)/shard_map/power_chain/pallas_call | solution.py:521
  97.7 11.0 %rebuild.1 = bf16[3584,3072]{1,0:T(8,128)(2,1)} custom-call(bf16[16,2,16,256]{3,2,1,0:T(8,128)(2,1)} %get-tuple-element.7.left_hbm, bf16[4,16,2,16,768]{4,3,2,1,0:T(8,128)(2,1)} %bitcast.3), custom_call_target="tpu_custom_call" | custom-call | tf_op jit(solution)/shard_map/rebuild/pallas_call | solution.py:561

commit v5 on v4

--- a/solution.py
+++ b/solution.py
@@ -11,9 +11,9 @@
 POWER = 2
 SIDE = 4
 LANES = 128
-GROUPS = 2
+GROUPS = 4
 CHUNKS = 4
-ROUNDS = (1, 1, 1, 1)
+ROUNDS = (2, 1, 1)
 CUT = None
 VMEM_BYTES = 60 * 1024 * 1024
 
@@ -414,7 +414,7 @@
         f2[col, row, g, :, pod] = f1[g, pod]
 
     row, col = rows_ring.place, cols_ring.place
-    row_k, cross_k, unit_k, far_k = take(len(SHIFTS)), take(1), take(2 * SIDE), take(1)
+    row_k, cross_k, unit_k, far_k = take(len(SHIFTS)), take(1), take(2 * SIDE), take(SIDE)
 
     chains = [piece_chain(g) for g in range(GROUPS)]
     waits = [lambda: None] * GROUPS
@@ -443,14 +443,22 @@
         def unit_start(slot, i):
             go(0, slot, 0, 1, unit_k + 2 * i)
             go(0, slot, 1, -1, unit_k + 2 * i + 1)
-            go(0, slot, 1, 1, far_k)
-            go(0, slot, 0, -1, far_k)
+            go(0, slot, 1, 1, far_k + i)
+            go(0, slot, 0, -1, far_k + i)
 
         def unit_forward(slot, i):
             came(f2.at[cols_ring.at(-1), slot, :, :, 0], unit_k + 2 * i)
-            go(-1, slot, 0, 1, far_k)
+            go(-1, slot, 0, 1, far_k + i)
             came(f2.at[cols_ring.at(1), slot, :, :, 1], unit_k + 2 * i + 1)
-            go(1, slot, 1, -1, far_k)
+            go(1, slot, 1, -1, far_k + i)
+
+        def unit_done(slot, i):
+            came(f2.at[pl.ds(0, 2), slot], far_k + i)
+            out = pltpu.make_async_copy(
+                f2.at[:, slot], right_out.at[:, slot], local_sems.at[5 + GROUPS + i]
+            )
+            out.start()
+            left_over.append(out.wait)
 
         came(f2.at[col, row, :, :, 1 - pod], cross_k)
         went(f2.at[col, row, :, :, 1 - pod], cross_k)
@@ -461,12 +469,12 @@
             came(f2.at[col, slots[-1]], row_k + i)
             unit_start(slots[-1], i + 1)
             unit_forward(slots[-2], i)
+            if i > 0:
+                unit_done(slots[i - 1], i - 1)
         unit_forward(slots[-1], SIDE - 1)
-        came(f2.at[pl.ds(0, 2)], far_k)
+        unit_done(slots[-2], SIDE - 2)
+        unit_done(slots[-1], SIDE - 1)
         went(f2.at[pl.ds(0, 3)], far_k)
-        out = pltpu.make_async_copy(f2, right_out, local_sems.at[5 + GROUPS])
-        out.start()
-        left_over.append(out.wait)
     for wait in left_over:
         wait()
 
@@ -517,7 +525,7 @@
     per_row = share // SIDE
     scale = 1.0 / math.sqrt(tokens * members)
     any_space = pl.BlockSpec(memory_space=pl.ANY)
-    sem_count = 6 + GROUPS * (POWER * 7 + 5) + 13
+    sem_count = 6 + GROUPS * (POWER * 7 + 5) + 16
     right_atoms, left_atoms = pl.pallas_call(
         functools.partial(chain, members, atoms, own_rows, scale),
         out_shape=(
@@ -551,7 +559,7 @@
             pltpu.VMEM((SIDE, SIDE, GROUPS, per_row, pods, atoms, quarter), BF16),
             pltpu.SemaphoreType.DMA((sem_count,)),
             pltpu.SemaphoreType.DMA((sem_count,)),
-            pltpu.SemaphoreType.DMA((6 + GROUPS,)),
+            pltpu.SemaphoreType.DMA((5 + GROUPS + SIDE,)),
         ],
         compiler_params=pltpu.CompilerParams(
             collective_id=0, has_side_effects=True, vmem_limit_bytes=VMEM_BYTES

time: 109 us -> 106 us (0.972)
  Pallas kernels: 108 us -> 105 us
    pallas_call x1, Pallas kernels: 97 us -> 93.6 us  [shards(): pl.pallas_call(functools.partial(chain, members, atoms, own_rows, scale),...]
where the time goes in v5:
time: 106 us; the launch traced here: 105 us
  Pallas kernels  105 us (99%)
    pallas_call x1, Pallas kernels, shards(): pl.pallas_call(functools.partial(chain, members, atoms, own_rows, scale),...  93.6 us
    pallas_call x1, Pallas kernels, shards(): pl.pallas_call(rebuild_kernel, out_shape=jax.ShapeDtypeStruct((hidden_row...  11 us

profile of v5, /device:TPU:1, one launch (start us, length us, event | category | flops | bytes accessed | tf_op | source)
XLA Modules:
  0.0 105.4 jit_solution(4588053242239701468)
XLA Ops:
  0.7 93.6 %power_chain.1 = (bf16[4,4,4,1,2,16,768]{6,5,4,3,2,1,0:T(8,128)(2,1)}, bf16[16,2,16,256]{3,2,1,0:T(8,128)(2,1)}) custom-call(bf16[256,3584]{1,0:T(8,128)(2,1)} %h_hbm.1, bf16[256,6144]{1,0:T(8,128)(2,1)} %o_hbm.1, f32[16,6144]{1,0:T(8,128)} %s_hbm.1, s32[1,1]{1,0:T(1,128)} %bitcast.2.kept_ref), custom_call_target="tpu_custom_call" | custom-call | tf_op jit(solution)/shard_map/power_chain/pallas_call | solution.py:529
  94.2 11.0 %rebuild.1 = bf16[3584,3072]{1,0:T(8,128)(2,1)} custom-call(bf16[16,2,16,256]{3,2,1,0:T(8,128)(2,1)} %get-tuple-element.7.left_hbm, bf16[4,16,2,16,768]{4,3,2,1,0:T(8,128)(2,1)} %bitcast.3), custom_call_target="tpu_custom_call" | custom-call | tf_op jit(solution)/shard_map/rebuild/pallas_call | solution.py:569

commit v6 on v5

--- a/solution.py
+++ b/solution.py
@@ -80,7 +80,7 @@
         return self.member(self.at(shift))
 
 
-SHIFTS = (1, 3, 2)
+SHIFTS = (2, 1, 3)
 
 
 def chain(

time: 106 us -> 105 us (level)
  no operation moved by 1% of the time
where the time goes in v6:
time: 105 us
  Pallas kernels  104 us (99%)
    pallas_call x1, Pallas kernels, shards(): pl.pallas_call(functools.partial(chain, members, atoms, own_rows, scale),...  93.3 us
    pallas_call x1, Pallas kernels, shards(): pl.pallas_call(rebuild_kernel, out_shape=jax.ShapeDtypeStruct((hidden_row...  11 us

profile of v6, /device:TPU:1, one launch (start us, length us, event | category | flops | bytes accessed | tf_op | source)
XLA Modules:
  0.0 105.1 jit_solution(10367733983719486870)
XLA Ops:
  0.7 93.3 %power_chain.1 = (bf16[4,4,4,1,2,16,768]{6,5,4,3,2,1,0:T(8,128)(2,1)}, bf16[16,2,16,256]{3,2,1,0:T(8,128)(2,1)}) custom-call(bf16[256,3584]{1,0:T(8,128)(2,1)} %h_hbm.1, bf16[256,6144]{1,0:T(8,128)(2,1)} %o_hbm.1, f32[16,6144]{1,0:T(8,128)} %s_hbm.1, s32[1,1]{1,0:T(1,128)} %bitcast.2.kept_ref), custom_call_target="tpu_custom_call" | custom-call | tf_op jit(solution)/shard_map/power_chain/pallas_call | solution.py:529
  94.0 11.0 %rebuild.1 = bf16[3584,3072]{1,0:T(8,128)(2,1)} custom-call(bf16[16,2,16,256]{3,2,1,0:T(8,128)(2,1)} %get-tuple-element.7.left_hbm, bf16[4,16,2,16,768]{4,3,2,1,0:T(8,128)(2,1)} %bitcast.3), custom_call_target="tpu_custom_call" | custom-call | tf_op jit(solution)/shard_map/rebuild/pallas_call | solution.py:569
